TPU v7x, 512 devices: a whole 4x4x16 slice. The times are simulated.
512 devices in a mesh: seq: 128 (over z, y, core), rep: 4 (over x).
Axes of the slice: x: 4, y: 4, z: 16, core: 2. Of those that a mesh axis runs over, the one named last changes fastest.
Arguments:
- points: bfloat16 [4, 131072, 128], P('rep', 'seq'), may hold values from -6 to 6
- grad_rows: bfloat16 [4, 131072, 128], P('rep', 'seq'), may hold values from -6 to 6
- order: int32 [4, 131072], P('rep', 'seq'), may hold values from 0 to 131071, as said below
- w_qkv: bfloat16 [128, 384], replicated, may hold values from -0.5 to 0.5
- w_out: bfloat16 [128, 128], replicated, may hold values from -0.5 to 0.5
- norm_gain: float32 [128], replicated, may hold values from 0.5 to 1.5
- conv_taps: float32 [7, 128], replicated, may hold values from -1.5 to 1.5
Outputs:
- grad_points: float32 [4, 131072, 128], P('rep', 'seq')
- grad_qkv: float32 [128, 384], replicated
- grad_wout: float32 [128, 128], replicated
- grad_gain: float32 [128], replicated
- grad_taps: float32 [7, 128], replicated
Inputs may be any that keep to these rules, and one draw needn't show every extreme that they name: Within each slab, order is a permutation of 0 to 131071. Take aligned blocks of 1024 points and of 1024 positions. The blocks of points map one to one onto the blocks of positions (each block of points has its own block of positions): each block of points sends exactly 4 rows to every other block of positions and its remaining 1024 - 127 * 4 rows to its own.
All inputs are finite; a program needn't handle non-finite values.
Results may differ from a plain program's by a relative error of at most 0.0075.
The roundings to bfloat16 on the way count: a program that leaves them out, or rounds other values in their place, can miss the bound.
Values may be sent and summed in bfloat16 or wider, within the bound.
A program may use at most 64 MiB of HBM per device.

v0:
```python
import jax
import jax.numpy as jnp
from jax import lax
from jax.sharding import PartitionSpec as P

HEADS = 8
PATCH = 1024


def with_halo(x, sides, width):
    for axis, dim in sides:
        count, length = (lax.axis_size(axis), x.shape[dim])
        up = [(i, (i + 1) % count) for i in range(count - 1)]
        down = [(j, i) for i, j in up]
        last = lax.slice_in_dim(x, length - width, length, axis=dim)
        initial = lax.slice_in_dim(x, 0, width, axis=dim)
        before = lax.ppermute(last, axis, up)
        after = lax.ppermute(initial, axis, down)
        x = jnp.concatenate([before, x, after], axis=dim)
    return x


def head_attend(query, keyset, values):
    scale = 1.0 / jnp.sqrt(jnp.float32(query.shape[1]))
    scores = jnp.einsum("qe,ke->qk", query, keyset, preferred_element_type=jnp.float32) * scale
    scores = scores - jnp.max(scores, axis=1, keepdims=True)
    expon = jnp.exp(scores)
    probs = (expon / jnp.sum(expon, axis=1, keepdims=True)).astype(jnp.bfloat16)
    return jnp.einsum("qk,ke->qe", probs, values, preferred_element_type=jnp.float32).astype(
        jnp.bfloat16
    )


def layer_forward(rows, w_qkv, w_out, norm_gain):
    count, width = rows.shape
    center = rows - jnp.mean(rows, axis=1, keepdims=True)
    spread = jnp.mean(center * center, axis=1, keepdims=True)
    normed = center * lax.rsqrt(spread + 1e-05) * norm_gain
    mixed = jnp.dot(
        normed.astype(jnp.bfloat16), w_qkv.astype(jnp.bfloat16), preferred_element_type=jnp.float32
    )
    split_heads = (
        mixed.astype(jnp.bfloat16).reshape(count, 3, HEADS, width // HEADS).transpose(1, 2, 0, 3)
    )
    attend_one = jax.checkpoint(lambda triple: head_attend(triple[0], triple[1], triple[2]))
    attended = lax.map(attend_one, (split_heads[0], split_heads[1], split_heads[2]))
    attended = attended.transpose(1, 0, 2).reshape(count, width)
    return rows + jnp.dot(attended, w_out.astype(jnp.bfloat16), preferred_element_type=jnp.float32)


def patch_grads(rows, cotangent, w_qkv, w_out, norm_gain):
    primal, pull = jax.vjp(
        layer_forward,
        rows.astype(jnp.float32),
        w_qkv.astype(jnp.float32),
        w_out.astype(jnp.float32),
        norm_gain,
    )
    return pull(cotangent.astype(jnp.float32))


def patch_sweep(patched, patch_grad, w_qkv, w_out, norm_gain):
    width = patched.shape[1]
    blocks = patched.reshape(-1, PATCH, width)
    cot_blocks = patch_grad.reshape(-1, PATCH, width)
    start = (
        jnp.zeros(w_qkv.shape, jnp.float32),
        jnp.zeros(w_out.shape, jnp.float32),
        jnp.zeros(norm_gain.shape, jnp.float32),
    )

    def advance(carry, pair):
        grads = patch_grads(pair[0], pair[1], w_qkv, w_out, norm_gain)
        carry = (carry[0] + grads[1], carry[1] + grads[2], carry[2] + grads[3])
        return (carry, grads[0].astype(jnp.bfloat16))

    totals, backs = lax.scan(advance, start, (blocks, cot_blocks))
    return (totals, backs.reshape(-1, width))


def body(points, grad_rows, order, w_qkv, w_out, norm_gain, conv_taps):
    local_pts = points[0]
    count, width = local_pts.shape
    taps = conv_taps.shape[0]
    reach = taps // 2
    shards = lax.axis_size("seq")
    spill_rows = count // (2 * shards)
    padded = with_halo(local_pts, (("seq", 0),), reach).astype(jnp.float32)
    encoded = local_pts.astype(jnp.float32)
    for offset in range(taps):
        encoded = encoded + conv_taps[offset] * padded[offset : offset + count]
    encoded = encoded.astype(jnp.bfloat16)
    targets = order[0]
    dest_block = targets // count
    within = targets % count
    shard_ids = jnp.arange(shards, dtype=jnp.int32)
    block_hits = (dest_block[:, None] == shard_ids[None, :]).astype(jnp.int32)
    main_block = jnp.argmax(jnp.sum(block_hits, axis=0))
    owners_all = lax.all_gather(main_block[None], "seq", axis=0, tiled=True)
    owner_of_block = jnp.sum(
        jnp.where(owners_all[None, :] == shard_ids[:, None], shard_ids[None, :], 0), axis=1
    )
    device_of_row = jnp.sum(block_hits * owner_of_block[None, :], axis=1)
    is_main = dest_block == main_block
    sort_key = jnp.where(is_main, shards, device_of_row)
    sorter = jnp.argsort(sort_key, stable=True)
    sorted_dev = sort_key[sorter]
    per_device = jnp.sum((sort_key[:, None] == shard_ids[None, :]).astype(jnp.int32), axis=0)
    starts = jnp.cumsum(per_device) - per_device
    row_start = jnp.sum(
        jnp.where(sorted_dev[:, None] == shard_ids[None, :], starts[None, :], 0), axis=1
    )
    rank = jnp.arange(count, dtype=jnp.int32) - row_start
    capacity = shards * spill_rows
    slot = jnp.where(sorted_dev < shards, sorted_dev * spill_rows + rank, capacity)
    enc_send = (
        jnp.zeros((capacity, width), jnp.bfloat16)
        .at[slot]
        .set(encoded[sorter], mode="drop")
        .reshape(shards, spill_rows, width)
    )
    cot_send = (
        jnp.zeros((capacity, width), jnp.bfloat16)
        .at[slot]
        .set(grad_rows[0][sorter], mode="drop")
        .reshape(shards, spill_rows, width)
    )
    pos_send = (
        jnp.full((capacity,), -1, jnp.int32)
        .at[slot]
        .set(within[sorter], mode="drop")
        .reshape(shards, spill_rows)
    )
    cot_recv, pos_recv = (
        lax.all_to_all(cot_send, "seq", split_axis=0, concat_axis=0, tiled=True),
        lax.all_to_all(pos_send, "seq", split_axis=0, concat_axis=0, tiled=True),
    )
    enc_recv = lax.all_to_all(enc_send, "seq", split_axis=0, concat_axis=0, tiled=True)
    pos_flat = pos_recv.reshape(capacity)
    recv_index = jnp.where(pos_flat >= 0, pos_flat, count)
    main_index = jnp.where(is_main, within, count)
    patched = jnp.zeros((count, width), jnp.bfloat16).at[main_index].set(encoded, mode="drop")
    patched = patched.at[recv_index].set(enc_recv.reshape(capacity, width), mode="drop")
    patch_grad = (
        jnp.zeros((count, width), jnp.bfloat16).at[main_index].set(grad_rows[0], mode="drop")
    )
    patch_grad = patch_grad.at[recv_index].set(cot_recv.reshape(capacity, width), mode="drop")
    totals, backs = patch_sweep(patched, patch_grad, w_qkv, w_out, norm_gain)
    back_send = backs[jnp.minimum(recv_index, count - 1)].reshape(shards, spill_rows, width)
    returned = lax.all_to_all(back_send, "seq", split_axis=0, concat_axis=0, tiled=True).reshape(
        capacity, width
    )
    spill_sorted = returned[jnp.minimum(slot, capacity - 1)]
    spill_back = jnp.zeros((count, width), jnp.bfloat16).at[sorter].set(spill_sorted)
    curve_back = jnp.where(is_main[:, None], backs[within], spill_back)
    back_float = curve_back.astype(jnp.float32)
    back_pad = with_halo(curve_back, (("seq", 0),), reach).astype(jnp.float32)
    grad_feats = back_float
    for offset in range(taps):
        grad_feats = (
            grad_feats
            + conv_taps[offset] * back_pad[2 * reach - offset : 2 * reach - offset + count]
        )
    tap_terms = jnp.stack(
        [jnp.sum(back_float * padded[offset : offset + count], axis=0) for offset in range(taps)]
    )
    sum_qkv, sum_out, sum_gain, sum_taps = lax.psum(
        (totals[0], totals[1], totals[2], tap_terms), ("seq", "rep")
    )
    return (grad_feats[None], sum_qkv, sum_out, sum_gain, sum_taps)


def solution(mesh):
    placed = (P("rep", "seq", None), P("rep", "seq", None), P("rep", "seq"), P(), P(), P(), P())
    return jax.shard_map(
        body,
        mesh=mesh,
        in_specs=placed,
        out_specs=(P("rep", "seq", None), P(), P(), P(), P()),
        check_vma=False,
    )
```

profile of v0, /device:TPU:1, one launch (start us, length us, event | category | flops | bytes accessed | tf_op | source)
XLA Modules:
  0.0 739.3 jit_solution(3550392894373352515)
XLA Ops:
  7.9 4.6 collective-permute-start
  12.5 5.5 collective-permute-start.1
  22.3 26.0 %all-reduce.3 = s32[128]{0:T(128)S(1)} all-reduce(s32[128]{0:T(128)S(1)} %dynamic-update-slice), channel_id=1, replica_groups=mesh['seq'=128,'rep'=4] {'seq'}, use_global_device_ids=true, to_apply=%add.3 | all-reduce | flops 128 | bytes 1024
  50.2 4.4 sort.17
  55.2 4.5 gather_fusion
  60.5 4.5 gather_fusion.1
  65.1 4.3 scatter_custom_fusion.1
  70.1 16.1 %all-to-all-start = ((s32[128,1,4]{2,1,0:T(1,128)}), s32[128,1,4]{2,1,0:T(1,128)S(1)}, u32[]{:S(2)}, u32[]{:S(2)}) async-start(s32[128,1,4]{2,1,0:T(1,128)} %bitcast.21), calls=%async_computation | async-start | bytes 131072 | tf_op jit(solution)/shard_map/all_to_all | solution.py:136
  87.5 6.8 scatter_custom_fusion.2
  94.4 6.7 all-to-all-done
  101.0 9.7 %all-to-all-start.1 = ((bf16[128,4,128]{2,1,0:T(4,128)(2,1)}), bf16[128,4,128]{2,1,0:T(4,128)(2,1)S(1)}, u32[]{:S(2)}, u32[]{:S(2)}) async-start(bf16[128,4,128]{2,1,0:T(4,128)(2,1)} %bitcast.23), calls=%async_computation.1 | async-start | bytes 262144 | tf_op jit(solution)/shard_map/all_to_all | solution.py:135
  110.8 3.2 scatter_custom_fusion
  115.4 6.8 scatter_custom_fusion.5
  122.3 3.2 scatter_custom_fusion.4
  127.0 16.1 %all-to-all-start.2 = ((bf16[128,4,128]{2,1,0:T(4,128)(2,1)}), bf16[128,4,128]{2,1,0:T(4,128)(2,1)S(1)}, u32[]{:S(2)}, u32[]{:S(2)}) async-start(bf16[128,4,128]{2,1,0:T(4,128)(2,1)} %bitcast.35), calls=%async_computation.2 | async-start | bytes 262144 | tf_op jit(solution)/shard_map/all_to_all | solution.py:138
  145.4 13.7 %all-to-all-done.2 = bf16[128,4,128]{2,1,0:T(4,128)(2,1)S(1)} async-done(((bf16[128,4,128]{2,1,0:T(4,128)(2,1)}), bf16[128,4,128]{2,1,0:T(4,128)(2,1)S(1)}, u32[]{:S(2)}, u32[]{:S(2)}) %all-to-all-start.2) | async-done | bytes 131104 | tf_op jit(solution)/shard_map/all_to_all | solution.py:138
  162.9 66.3 %while.43 = (s32[]{:T(128)}, bf16[8,1024,16]{1,2,0:T(8,128)(2,1)S(1)}, bf16[8,1024,16]{1,2,0:T(8,128)(2,1)S(1)}, bf16[8,1024,16]{1,2,0:T(8,128)(2,1)}, bf16[8,10...) while((s32[]{:T(128)}, ...), condition=%wide.region_23.24_spmd, body=%wide.region_17.23_spmd.sunk | while | flops 201375744 | bytes 41574532 | solution.py:46
  233.8 7.1 all-to-all-start.3
  241.3 25.1 %while.44 = (s32[]{:T(128)}, bf16[8,1024,16]{1,2,0:T(8,128)(2,1)S(1)}, bf16[8,1024,16]{1,2,0:T(8,128)(2,1)S(1)}, bf16[8,1024,16]{1,2,0:T(8,128)(2,1)S(1)}, bf16[8,1024,16]{1,2,0:T(8,128)(2,1)}, /*index=5*/s32[]{:T(128)}) while((s32[]{:T(128)}, bf16[8,1024,16]{1,2,0:T(8,128)(2,1)S(1)}, bf16[8,1024,16]{1,2,0:T(8,128)(2,1)S(1)}, ...), condition=%wide.region_31.32_spmd, body=%wide.region_28.31_spmd.sunk | while | flops 76560384 | bytes 12736581 | solution.py:46
  266.4 3.2 gather_fusion.2
  271.6 6.4 scatter_custom_fusion.7
  278.6 3.5 collective-permute-start.2
  284.1 106.1 %all-reduce.4 = (f32[128]{0:T(128)}, f32[7,128]{1,0:T(8,128)}) all-reduce(f32[128]{0:T(128)S(1)} %get-tuple-element.241, f32[7,128]{1,0:T(8,128)S(1)} %stack.31), channel_id=1, replica_groups=mesh['seq'=128,'rep'=4] {'seq','rep'}, use_global_device_ids=true, to_apply=%region_34.35 | all-reduce | flops 1024 | bytes 8192 | tf_op jit(solution)/shard_map/psum | solution.py:167
  392.3 336.6 %all-reduce.8.cloned.1.call-done = (f32[128,384]{1,0:T(8,128)}, f32[128,128]{1,0:T(8,128)}) async-done(((f32[128,384]{1,0:T(8,128)}, f32[128,128]{1,0:T(8,128)}), (f32[128,384]{1,0:T(8,128)}, f32[128,128]{1,0:T(8,128)})) %all-reduce.8.cloned.1.call-update) | async-done | bytes 262160 | tf_op jit(solution)/shard_map/psum | solution.py:167
  (224 shorter events, 124.6 us)
Async XLA Ops:
  7.2 80.4 %copy-start = (bf16[1,1024,128]{2,1,0:T(8,128)(2,1)S(1)}, bf16[1,1024,128]{2,1,0:T(8,128)(2,1)}, u32[]{:S(2)}) copy-start(bf16[1,1024,128]{2,1,0:T(8,128)(2,1)} %param.12) | copy-start | bytes 786436
  7.9 106.1 %collective-permute-start = (bf16[3,128]{1,0:T(4,128)(2,1)S(1)}, bf16[3,128]{1,0:T(4,128)(2,1)S(1)}, u32[]{:S(2)}, u32[]{:S(2)}) collective-permute-start(bf16[3,128]{1,0:T(4,128)(2,1)S(1)} %get-tuple-element.307), channel_id=1, source_target_pairs={{0,4},{4,8},{8,12},{12,16},{16,20},{20,24},{24,28},{28,32},{32,36}... | collective-permute-start | bytes 2312 | tf_op jit(solution)/shard_map/ppermute | solution.py:17
  12.5 101.5 %collective-permute-start.1 = (bf16[3,128]{1,0:T(4,128)(2,1)S(1)}, bf16[3,128]{1,0:T(4,128)(2,1)S(1)}, u32[]{:S(2)}, u32[]{:S(2)}) collective-permute-start(bf16[3,128]{1,0:T(4,128)(2,1)S(1)} %get-tuple-element.306), channel_id=1, source_target_pairs={{4,0},{8,4},{12,8},{16,12},{20,16},{24,20},{28,24},{32,28},{36,32}... | collective-permute-start | bytes 2312 | tf_op jit(solution)/shard_map/ppermute | solution.py:18
  55.2 31.1 %copy-start.4 = (s32[1,1024]{1,0:T(1,128)S(1)}, s32[1,1024]{1,0:T(1,128)}, u32[]{:S(2)}) copy-start(s32[1,1024]{1,0:T(1,128)} %param.13) | copy-start | bytes 12292
  55.2 55.6 %copy-start.12 = (f32[7,128]{1,0:T(8,128)S(1)}, f32[7,128]{1,0:T(8,128)}, u32[]{:S(2)}) copy-start(f32[7,128]{1,0:T(8,128)} %param.17) | copy-start | bytes 10756
  55.2 58.9 %copy-start.1 = (bf16[1,1024,128]{2,1,0:T(8,128)(2,1)S(1)}, bf16[1,1024,128]{2,1,0:T(8,128)(2,1)}, u32[]{:S(2)}) copy-start(bf16[1,1024,128]{2,1,0:T(8,128)(2,1)} %param.11) | copy-start | bytes 786436
  70.1 30.9 %all-to-all-start = ((s32[128,1,4]{2,1,0:T(1,128)}), s32[128,1,4]{2,1,0:T(1,128)S(1)}, u32[]{:S(2)}, u32[]{:S(2)}) async-start(s32[128,1,4]{2,1,0:T(1,128)} %bitcast.21), calls=%async_computation | async-start | bytes 131072 | tf_op jit(solution)/shard_map/all_to_all | solution.py:136
  101.0 25.9 %all-to-all-start.1 = ((bf16[128,4,128]{2,1,0:T(4,128)(2,1)}), bf16[128,4,128]{2,1,0:T(4,128)(2,1)S(1)}, u32[]{:S(2)}, u32[]{:S(2)}) async-start(bf16[128,4,128]{2,1,0:T(4,128)(2,1)} %bitcast.23), calls=%async_computation.1 | async-start | bytes 262144 | tf_op jit(solution)/shard_map/all_to_all | solution.py:135
  110.8 4.1 copy-start.9
  110.8 15.2 %copy-start.7 = (f32[128]{0:T(128)}, f32[128]{0:T(128)S(1)}, u32[]{:S(2)}) copy-start(f32[128]{0:T(128)S(1)} %get-tuple-element.315) | copy-start | bytes 1540
  114.9 30.3 %copy-start.5 = (bf16[128,128]{1,0:T(8,128)(2,1)S(1)}, bf16[128,128]{1,0:T(8,128)(2,1)}, u32[]{:S(2)}) copy-start(bf16[128,128]{1,0:T(8,128)(2,1)} %param.15) | copy-start | bytes 98308
  115.4 46.2 %copy-start.3 = (bf16[128,384]{1,0:T(8,128)(2,1)S(1)}, bf16[128,384]{1,0:T(8,128)(2,1)}, u32[]{:S(2)}) copy-start(bf16[128,384]{1,0:T(8,128)(2,1)} %param.14) | copy-start | bytes 294916
  115.4 46.2 %copy-start.6 = (f32[128]{0:T(128)S(1)}, f32[128]{0:T(128)}, u32[]{:S(2)}) copy-start(f32[128]{0:T(128)} %param.16) | copy-start | bytes 1540
  127.0 32.2 %all-to-all-start.2 = ((bf16[128,4,128]{2,1,0:T(4,128)(2,1)}), bf16[128,4,128]{2,1,0:T(4,128)(2,1)S(1)}, u32[]{:S(2)}, u32[]{:S(2)}) async-start(bf16[128,4,128]{2,1,0:T(4,128)(2,1)} %bitcast.35), calls=%async_computation.2 | async-start | bytes 262144 | tf_op jit(solution)/shard_map/all_to_all | solution.py:138
  229.2 0.7 copy-start.2
  233.8 37.7 %all-to-all-start.3 = ((bf16[128,4,128]{2,1,0:T(4,128)(2,1)}), bf16[128,4,128]{2,1,0:T(4,128)(2,1)S(1)}, u32[]{:S(2)}, u32[]{:S(2)}) async-start(bf16[128,4,128]{2,1,0:T(4,128)(2,1)} %bitcast.52), calls=%async_computation.3 | async-start | bytes 262144 | tf_op jit(solution)/shard_map/all_to_all | solution.py:150
  241.0 488.0 %all-reduce.8.cloned.1.call-start = ((), (), s32[]{:S(2)}) async-start(), calls=%async_computation.4 | async-start | bytes 524288 | tf_op jit(solution)/shard_map/psum | solution.py:167
  266.4 11.6 %copy-start.11 = (pred[1024]{0:T(1024)(128)(4,1)S(1)}, pred[1024]{0:T(1024)(128)(4,1)}, u32[]{:S(2)}) copy-start(pred[1024]{0:T(1024)(128)(4,1)} %get-tuple-element.290) | copy-start | bytes 3076
  269.6 121.5 %copy-start.8 = (f32[128]{0:T(128)S(1)}, f32[128]{0:T(128)}, u32[]{:S(2)}) copy-start(f32[128]{0:T(128)} %copy-done.7) | copy-start | bytes 1540
  269.6 121.5 %copy-start.10 = (f32[128]{0:T(128)S(1)}, f32[128]{0:T(128)}, u32[]{:S(2)}) copy-start(f32[128]{0:T(128)} %copy-done.9) | copy-start | bytes 1540
  278.6 111.6 %collective-permute-start.2 = (bf16[3,128]{1,0:T(4,128)(2,1)S(1)}, bf16[3,128]{1,0:T(4,128)(2,1)S(1)}, u32[]{:S(2)}, u32[]{:S(2)}) collective-permute-start(bf16[3,128]{1,0:T(4,128)(2,1)S(1)} %get-tuple-element.305), channel_id=1, source_target_pairs={{0,4},{4,8},{8,12},{12,16},{16,20},{20,24},{24,28},{28,32},{32,36}... | collective-permute-start | bytes 2312 | tf_op jit(solution)/shard_map/ppermute | solution.py:17
  282.2 108.0 %collective-permute-start.3 = (bf16[3,128]{1,0:T(4,128)(2,1)S(1)}, bf16[3,128]{1,0:T(4,128)(2,1)S(1)}, u32[]{:S(2)}, u32[]{:S(2)}) collective-permute-start(bf16[3,128]{1,0:T(4,128)(2,1)S(1)} %get-tuple-element.304), channel_id=1, source_target_pairs={{4,0},{8,4},{12,8},{16,12},{20,16},{24,20},{28,24},{32,28},{36,32}... | collective-permute-start | bytes 2312 | tf_op jit(solution)/shard_map/ppermute | solution.py:18
Sparse Core Ops, SparseCore 0:
  271.7 457.2 all-reduce.7
where the time goes:
time: 749 us; the launch traced here: 739 us
  waiting for transfers between devices  357 us (48%)
  blocking collectives  132 us (18%)
  matrix products  71.7 us (10%)
  starting transfers between devices  64.9 us (9%)
  local copies, waits for them, and re-layouts  60.9 us (8%)
  other arithmetic  37.2 us (5%)
  between operations  15 us (2%)
    psum x1, waiting for transfers between devices, body(): lax.psum((totals[0], totals[1], totals[2], tap_terms), ('seq', 'rep'))  337 us
    psum x1, blocking collectives, body(): lax.psum((totals[0], totals[1], totals[2], tap_terms), ('seq', 'rep'))  106 us
    dot_general x24, matrix products, head_attend(): jnp.einsum('qk,ke->qe', probs, values, preferred_element_type=jnp.float32)  42.7 us
    dot_general x32, matrix products, head_attend(): jnp.einsum('qe,ke->qk', query, keyset, preferred_element_type=jnp.float32)  26.1 us
    unnamed x1, blocking collectives  26 us
    all_to_all x1, starting transfers between devices, body(): lax.all_to_all(enc_send, 'seq', split_axis=0, concat_axis=0, tiled=True)  16.1 us
    all_to_all x1, starting transfers between devices, body(): lax.all_to_all(pos_send, 'seq', split_axis=0, concat_axis=0, tiled=True)  16.1 us
  transfers between devices with their start and end apart: 9, of which 3 were waited for; matrix products, arithmetic and copies ran while one was open for 12% of the time, Pallas kernels for 0%

commit v1 on v0

v1 whole, which is shorter than its diff:
```python
import functools

import jax
import jax.numpy as jnp
from jax import lax
from jax.experimental import pallas as pl
from jax.experimental.pallas import tpu as pltpu
from jax.sharding import PartitionSpec as P

F32 = jnp.float32
BF = jnp.bfloat16
MESH = pl.DeviceIdType.MESH
HEADS = 8
HALF = 512
ROWS = 1024
WIDTH = 128
NZ = 16
NYC = 8
NX = 4
NW = NX * NYC
SEQ = NZ * NYC


def dot(a, b):
    return jnp.dot(a, b, preferred_element_type=F32)


def ntdot(a, b):
    return lax.dot_general(a, b, (((1,), (1,)), ((), ())), preferred_element_type=F32)


def iota(shape, dim):
    return lax.broadcasted_iota(jnp.int32, shape, dim)


def hot(cond):
    return jnp.where(cond, 1.0, 0.0).astype(BF)


def kernel(
    pts_ref, cot_ref, order_ref, wqkv_ref, wout_ref, gain_ref, taps_ref,
    gp_ref, gq_ref, gw_ref, gg_ref, gt_ref,
    pp, pb, pbt, pret, q4, mine, agz, agw, scot, senc,
    tx, rx, bt, rr, patch, cotp,
    qT, kT, vT, doT, kf, vf, attT, dqT, dkT, dvT, xhT, rs, nbT, sbuf, eb, xb, w1, mref,
    cpad, acc, rsb, part, zb, full, fin, tmine, tw, tsum, tz,
    ssem, rsem,
):
    me = lax.axis_index("seq")
    rep = lax.axis_index("rep")
    z = me // NYC
    yc = lax.rem(me, NYC)
    w = rep * NYC + yc
    sig = yc * NZ + z

    def z_peer(t):
        zz = lax.rem(z + 1 + t, NZ)
        return zz, (zz * NYC + yc, rep)

    def yc_peer(t):
        cc = lax.rem(yc + 1 + t, NYC)
        return cc, (z * NYC + cc, rep)

    def w_peer(t):
        ww = lax.rem(w + 1 + t, NW)
        return ww, (z * NYC + lax.rem(ww, NYC), ww // NYC)

    def seq_peer(t):
        dd = lax.rem(me + 1 + t, SEQ)
        return lax.rem(dd, NYC) * NZ + dd // NYC, (dd, rep)

    nxt = (lax.rem(me + 1, SEQ), rep)
    prv = (lax.rem(me + SEQ - 1, SEQ), rep)

    def push(src, dst, k, dev):
        pltpu.make_async_remote_copy(
            src_ref=src, dst_ref=dst, send_sem=ssem.at[k], recv_sem=rsem.at[k],
            device_id=dev, device_id_type=MESH,
        ).start()

    def loop(count, step):
        def body(t, carry):
            step(t)
            return carry

        lax.fori_loop(0, count, body, 0)

    def wait_in(ref, k):
        pltpu.make_async_copy(ref, ref, rsem.at[k]).wait()

    def wait_out(ref, k):
        pltpu.make_async_copy(ref, ref, ssem.at[k]).wait()

    barrier = pltpu.get_barrier_semaphore()

    def greet(dev):
        pl.semaphore_signal(barrier, inc=1, device_id=dev, device_id_type=MESH)

    loop(NZ - 1, lambda t: greet(z_peer(t)[1]))
    loop(NW - 1, lambda t: greet(w_peer(t)[1]))
    greet(nxt)
    greet(prv)

    pp[8 : 8 + ROWS, :] = pts_ref[0].astype(F32)
    dest = order_ref[...] // ROWS
    blocks = iota((SEQ, ROWS), 0)
    hits = jnp.where(blocks == dest, 1.0, 0.0)
    counts = jnp.sum(hits, axis=1, keepdims=True)
    is_main = jnp.where(counts > 4.5, 1.0, 0.0)
    main = jnp.sum(is_main * iota((SEQ, 1), 0).astype(F32), axis=0, keepdims=True)
    mine[...] = jnp.broadcast_to(main, (1, WIDTH))
    pb[...] = hot(iota((ROWS, ROWS), 0) < iota((ROWS, ROWS), 1))
    before = dot(hits.astype(BF), pb[...])
    rank = jnp.sum(hits * before, axis=0, keepdims=True)
    main_row = jnp.sum(hits * is_main, axis=0, keepdims=True)
    slot = jnp.where(
        (main_row > 0.5) & (rank > 3.5),
        rank + float(HALF - 4),
        dest.astype(F32) * 4.0 + rank,
    )
    pb[...] = hot(iota((ROWS, ROWS), 0).astype(F32) == slot)
    slot_col = jnp.broadcast_to(slot, (8, ROWS)).T[:, 0:1]
    pbt[...] = hot(iota((ROWS, ROWS), 1).astype(F32) == slot_col)
    scot[...] = dot(pb[...], cot_ref[0]).astype(BF)
    eye = hot(iota((WIDTH, WIDTH), 0) == iota((WIDTH, WIDTH), 1))
    wq = wqkv_ref[...]
    wqT = jnp.concatenate(
        [wq[:, j * WIDTH : (j + 1) * WIDTH].astype(F32).T.astype(BF) for j in range(3)], axis=0
    )

    pl.semaphore_wait(barrier, NZ - 1 + NW - 1 + 2)

    def send_z(t):
        push(mine, agz.at[z], 0, z_peer(t)[1])

    loop(NZ - 1, send_z)
    push(pp.at[pl.ds(ROWS, 8)], pp.at[pl.ds(0, 8)], 1, nxt)
    push(pp.at[pl.ds(8, 8)], pp.at[pl.ds(ROWS + 8, 8)], 2, prv)
    agz[z] = mine[...]
    wait_in(agz.at[pl.ds(0, NZ - 1)], 0)

    def send_yc(t):
        push(agz, agw.at[yc], 3, yc_peer(t)[1])

    loop(NYC - 1, send_yc)
    agw[yc] = agz[...]
    wait_in(pp.at[pl.ds(0, 8)], 1)
    wait_in(pp.at[pl.ds(ROWS + 8, 8)], 2)
    has_prev = jnp.where(me > 0, 1.0, 0.0)
    has_next = jnp.where(me < SEQ - 1, 1.0, 0.0)
    wait_out(pp.at[pl.ds(ROWS, 8)], 1)
    wait_out(pp.at[pl.ds(8, 8)], 2)
    pp[0:8, :] = pp[0:8, :] * has_prev
    pp[ROWS + 8 : ROWS + 16, :] = pp[ROWS + 8 : ROWS + 16, :] * has_next
    enc = pp[8 : 8 + ROWS, :]
    for t in range(7):
        enc = enc + taps_ref[t : t + 1, :] * pp[5 + t : 5 + t + ROWS, :]
    senc[...] = dot(pb[...], enc.astype(BF)).astype(BF)
    wait_in(agw.at[pl.ds(0, NYC - 1)], 3)
    owners = agw[...].reshape(SEQ, WIDTH)
    pick = hot(owners == iota((SEQ, WIDTH), 1).astype(F32))
    grow = hot(iota((HALF, SEQ), 0) // 4 == iota((HALF, SEQ), 1))
    wide = ntdot(dot(grow, pick).astype(BF), grow)
    same = (iota((HALF, HALF), 0) % 4) == (iota((HALF, HALF), 1) % 4)
    q4[...] = jnp.where(same, wide, 0.0).astype(BF)
    tx[:, 0:4, :] = dot(q4[...], senc[0:HALF, :]).astype(BF).reshape(SEQ, 4, WIDTH)
    tx[:, 4:8, :] = dot(q4[...], scot[0:HALF, :]).astype(BF).reshape(SEQ, 4, WIDTH)

    def send_rows(t):
        slot_of, dev = seq_peer(t)
        push(tx.at[slot_of], rx.at[sig], 4, dev)

    loop(SEQ - 1, send_rows)
    rx[sig] = tx[sig]
    pret[...] = ntdot(pbt[:, 0:HALF], q4[...]).astype(BF)
    patch[HALF:, :] = senc[HALF:, :]
    cotp[HALF:, :] = scot[HALF:, :]
    gain = gain_ref[...]
    gainc = jnp.sum(jnp.where(eye.astype(F32) > 0.5, gain, 0.0), axis=1, keepdims=True)
    wait_in(rx.at[pl.ds(0, SEQ - 1)], 4)
    patch[0:HALF, :] = rx[:, 0:4, :].reshape(HALF, WIDTH)
    cotp[0:HALF, :] = rx[:, 4:8, :].reshape(HALF, WIDTH)

    xT = ntdot(eye, patch[...])
    center = xT - jnp.mean(xT, axis=0, keepdims=True)
    r = lax.rsqrt(jnp.mean(center * center, axis=0, keepdims=True) + 1e-5)
    xh = center * r
    xhT[...] = xh
    rs[...] = jnp.broadcast_to(r, rs.shape)
    nT = (xh * gainc).astype(BF)
    nbT[...] = nT
    mixed = dot(wqT, nT)
    qkvT = mixed.astype(BF)
    qT[...] = qkvT[0:128] * jnp.asarray(0.25, BF)
    kT[...] = qkvT[128:256]
    vT[...] = qkvT[256:384]
    kf[...] = mixed[128:256].T.astype(BF)
    vf[...] = mixed[256:384].T.astype(BF)
    doT[...] = ntdot(wout_ref[...], cotp[...]).astype(BF)
    ones = jnp.ones((16, ROWS), BF)
    for h in range(HEADS):
        w1[h * 48 : h * 48 + 16, :] = qkvT[256 + h * 16 : 272 + h * 16]
        w1[h * 48 + 16 : h * 48 + 32, :] = ones
        w1[h * 48 + 32 : h * 48 + 48, :] = qkvT[128 + h * 16 : 144 + h * 16]
    head_of = iota((WIDTH, ROWS), 0) // 16

    def masked(ref, h):
        return jnp.where(head_of == h, ref[...].astype(F32), 0.0).astype(BF)

    first = dot(kf[...], masked(qT, 0))
    sbuf[0] = first
    mref[0] = jnp.broadcast_to(jnp.max(first, axis=0, keepdims=True), (8, ROWS))

    def head(h, cur, other, last):
        hs = pl.ds(pl.multiple_of(h * 16, 16), 16)
        if not last:
            q_next = masked(qT, h + 1)
        do_wide = masked(doT, h)
        top = mref[cur][0:1, :]
        top_next = None
        for c in range(4):
            ks = slice(c * 256, c * 256 + 256)
            if not last:
                s = dot(kf[ks, :], q_next)
                sbuf[other, ks, :] = s
                high = jnp.max(s, axis=0, keepdims=True)
                top_next = high if top_next is None else jnp.maximum(top_next, high)
            e = jnp.exp(sbuf[cur, ks, :] - top)
            t = dot(vf[ks, :], do_wide)
            eb[ks, :] = e.astype(BF)
            xb[ks, :] = (e * t).astype(BF)
        if not last:
            mref[other] = jnp.broadcast_to(top_next, (8, ROWS))
        a = dot(w1[pl.ds(pl.multiple_of(h * 48, 16), 48), :], eb[...])
        inv = 1.0 / a[16:17]
        o = a[0:16] * inv
        attT[hs, :] = o.astype(BF)
        kx = dot(kT[hs, :], xb[...])
        do = doT[hs, :].astype(F32)
        q = qT[hs, :].astype(F32)
        delta = jnp.sum(do * o, axis=0, keepdims=True)
        dqT[hs, :] = ((kx - delta * a[32:48]) * (inv * 0.25)).astype(BF)
        back = ntdot(jnp.concatenate([do * inv, q * (-delta * inv)], axis=0).astype(BF), eb[...])
        dk = ntdot((q * inv).astype(BF), xb[...])
        dvT[hs, :] = back[0:16].astype(BF)
        dkT[hs, :] = (dk + back[16:32]).astype(BF)

    def pair(i, carry):
        head(2 * i, 0, 1, False)
        head(2 * i + 1, 1, 0, False)
        return carry

    lax.fori_loop(0, HEADS // 2 - 1, pair, 0)
    head(HEADS - 2, 0, 1, False)
    head(HEADS - 1, 1, 0, True)

    dall = jnp.concatenate([dqT[...], dkT[...], dvT[...]], axis=0)
    dnT = dot(wq, dall).astype(BF).astype(F32)
    xh = xhT[...]
    dxh = dnT * gainc
    m1 = jnp.mean(dxh, axis=0, keepdims=True)
    m2 = jnp.mean(dxh * xh, axis=0, keepdims=True)
    dxT = (dxh - m1 - xh * m2) * rs[0:1, :]
    patch[...] = (dxT.T + cotp[...].astype(F32)).astype(BF)
    bt[...] = patch[0:HALF, :].reshape(SEQ, 4, WIDTH)

    def send_back(t):
        slot_of, dev = seq_peer(t)
        push(bt.at[slot_of], rr.at[sig], 5, dev)

    loop(SEQ - 1, send_back)
    rr[sig] = bt[sig]

    ggT = jnp.sum(dnT * xh, axis=1, keepdims=True)
    gain_row = jnp.sum(jnp.where(eye.astype(F32) > 0.5, ggT, 0.0), axis=0, keepdims=True)
    for j in range(3):
        acc[j * 8 : j * 8 + 8] = ntdot(nbT[...], dall[j * WIDTH : (j + 1) * WIDTH]).reshape(8, 16, WIDTH)
    acc[24:32] = dot(attT[...], cotp[...]).reshape(8, 16, WIDTH)

    def send_part(t):
        ww, dev = w_peer(t)
        push(acc.at[ww], rsb.at[w], 6, dev)

    loop(NW - 1, send_part)
    rsb[w] = acc[w]
    own = dot(pbt[:, HALF:], patch[HALF:, :])
    wait_in(rsb.at[pl.ds(0, NW - 1)], 6)
    part[...] = jnp.sum(rsb[...], axis=0)

    def send_part_z(t):
        push(part, zb.at[z], 7, z_peer(t)[1])

    loop(NZ - 1, send_part_z)
    zb[z] = part[...]

    wait_in(rr.at[pl.ds(0, SEQ - 1)], 5)
    cb = own + dot(pret[...], rr[...].reshape(HALF, WIDTH))
    cpad[8 : 8 + ROWS, :] = cb
    push(cpad.at[pl.ds(ROWS, 8)], cpad.at[pl.ds(0, 8)], 8, nxt)
    push(cpad.at[pl.ds(8, 8)], cpad.at[pl.ds(ROWS + 8, 8)], 9, prv)
    tap_rows = [jnp.sum(cb * pp[5 + t : 5 + t + ROWS, :], axis=0, keepdims=True) for t in range(7)]
    tmine[...] = jnp.concatenate(tap_rows + [gain_row], axis=0)

    def send_tap(t):
        push(tmine, tw.at[w], 10, w_peer(t)[1])

    loop(NW - 1, send_tap)
    tw[w] = tmine[...]

    wait_in(zb.at[pl.ds(0, NZ - 1)], 7)
    full[...] = jnp.sum(zb[...], axis=0)

    def send_full(t):
        push(full, fin.at[w], 11, w_peer(t)[1])

    loop(NW - 1, send_full)
    fin[w] = full[...]

    wait_in(tw.at[pl.ds(0, NW - 1)], 10)
    tsum[...] = jnp.sum(tw[...], axis=0)

    def send_tap_z(t):
        push(tsum, tz.at[z], 12, z_peer(t)[1])

    loop(NZ - 1, send_tap_z)
    tz[z] = tsum[...]

    wait_in(cpad.at[pl.ds(0, 8)], 8)
    wait_in(cpad.at[pl.ds(ROWS + 8, 8)], 9)
    wait_out(cpad.at[pl.ds(ROWS, 8)], 8)
    wait_out(cpad.at[pl.ds(8, 8)], 9)
    cpad[0:8, :] = cpad[0:8, :] * has_prev
    cpad[ROWS + 8 : ROWS + 16, :] = cpad[ROWS + 8 : ROWS + 16, :] * has_next
    res = cpad[8 : 8 + ROWS, :]
    for t in range(7):
        res = res + taps_ref[t : t + 1, :] * cpad[11 - t : 11 - t + ROWS, :]
    gp_ref[0] = res

    wait_in(fin.at[pl.ds(0, NW - 1)], 11)
    for j in range(3):
        gq_ref[:, j * WIDTH : (j + 1) * WIDTH] = fin[j * 8 : j * 8 + 8].reshape(WIDTH, WIDTH)
    gw_ref[...] = fin[24:32].reshape(WIDTH, WIDTH)
    wait_in(tz.at[pl.ds(0, NZ - 1)], 12)
    total = jnp.sum(tz[...], axis=0)
    gt_ref[...] = total[0:7]
    gg_ref[...] = total[7:8]

    wait_out(agz.at[pl.ds(0, NZ - 1)], 0)
    wait_out(agw.at[pl.ds(0, NYC - 1)], 3)
    wait_out(rx.at[pl.ds(0, SEQ - 1)], 4)
    wait_out(rr.at[pl.ds(0, SEQ - 1)], 5)
    wait_out(rsb.at[pl.ds(0, NW - 1)], 6)
    wait_out(zb.at[pl.ds(0, NZ - 1)], 7)
    wait_out(tw.at[pl.ds(0, NW - 1)], 10)
    wait_out(fin.at[pl.ds(0, NW - 1)], 11)
    wait_out(tz.at[pl.ds(0, NZ - 1)], 12)


def body(points, grad_rows, order, w_qkv, w_out, norm_gain, conv_taps):
    def vm(shape, dtype):
        return pltpu.VMEM(shape, dtype)

    sq = (ROWS, ROWS)
    wide = (WIDTH, ROWS)
    tall = (ROWS, WIDTH)
    scratch = [
        vm((ROWS + 16, WIDTH), F32), vm(sq, BF), vm(sq, BF), vm((ROWS, HALF), BF), vm((HALF, HALF), BF),
        vm((1, WIDTH), F32), vm((NZ, 1, WIDTH), F32), vm((NYC, NZ, 1, WIDTH), F32), vm(tall, BF), vm(tall, BF),
        vm((SEQ, 8, WIDTH), BF), vm((SEQ, 8, WIDTH), BF), vm((SEQ, 4, WIDTH), BF), vm((SEQ, 4, WIDTH), BF),
        vm(tall, BF), vm(tall, BF),
        vm(wide, BF), vm(wide, BF), vm(wide, BF), vm(wide, BF), vm(tall, BF), vm(tall, BF),
        vm(wide, BF), vm(wide, BF), vm(wide, BF), vm(wide, BF), vm(wide, F32), vm((8, ROWS), F32), vm(wide, BF),
        vm((2,) + sq, F32), vm(sq, BF), vm(sq, BF), vm((HEADS * 48, ROWS), BF), vm((2, 8, ROWS), F32),
        vm((ROWS + 16, WIDTH), F32), vm((NW, 16, WIDTH), F32), vm((NW, 16, WIDTH), F32), vm((16, WIDTH), F32),
        vm((NZ, 16, WIDTH), F32), vm((16, WIDTH), F32), vm((NW, 16, WIDTH), F32),
        vm((8, WIDTH), F32), vm((NW, 8, WIDTH), F32), vm((8, WIDTH), F32), vm((NZ, 8, WIDTH), F32),
        pltpu.SemaphoreType.DMA((13,)), pltpu.SemaphoreType.DMA((13,)),
    ]
    spec = pl.BlockSpec(memory_space=pltpu.VMEM)
    shape = jax.ShapeDtypeStruct
    gp, gq, gw, gg, gt = pl.pallas_call(
        kernel,
        out_shape=(
            shape((1, ROWS, WIDTH), F32), shape((WIDTH, 3 * WIDTH), F32), shape((WIDTH, WIDTH), F32),
            shape((1, WIDTH), F32), shape((7, WIDTH), F32),
        ),
        in_specs=[spec] * 7,
        out_specs=[spec] * 5,
        scratch_shapes=scratch,
        compiler_params=pltpu.CompilerParams(
            collective_id=0, has_side_effects=True, vmem_limit_bytes=56 * 2**20
        ),
    )(points, grad_rows, order, w_qkv, w_out, norm_gain.reshape(1, WIDTH), conv_taps)
    return gp, gq, gw, gg.reshape(WIDTH), gt


def solution(mesh):
    placed = (P("rep", "seq", None), P("rep", "seq", None), P("rep", "seq"), P(), P(), P(), P())
    return jax.shard_map(
        body,
        mesh=mesh,
        in_specs=placed,
        out_specs=(P("rep", "seq", None), P(), P(), P(), P()),
        check_vma=False,
    )
```

time: 749 us -> 107 us (0.14); the launches traced: 739 us -> 107 us
  waiting for transfers between devices: 357 us -> 0 us
  blocking collectives: 132 us -> 0 us
  Pallas kernels: 0 us -> 102 us
  matrix products: 71.7 us -> 0 us
  starting transfers between devices: 64.9 us -> 0 us
  local copies, waits for them, and re-layouts: 60.9 us -> 4.52 us
  other arithmetic: 37.2 us -> 0 us
  between operations: 15 us -> 0.66 us
    psum x1 -> x0, waiting for transfers between devices: 337 us -> none  [body(): lax.psum((totals[0], totals[1], totals[2], tap_terms), ('seq', 'rep'))]
    psum x1 -> x0, blocking collectives: 106 us -> none  [body(): lax.psum((totals[0], totals[1], totals[2], tap_terms), ('seq', 'rep'))]
    pallas_call x0 -> x1, Pallas kernels: none -> 102 us  [body(): pl.pallas_call(kernel, out_shape=(shape((1, ROWS, WIDTH), F32), shape((WI...]
    dot_general x61 -> x0, matrix products: 71.7 us -> none  [the longest x24 42.7 us: head_attend(): jnp.einsum('qk,ke->qe', probs, values, preferred_element_type=jnp.float32)]
    all_to_all x4 -> x0, starting transfers between devices: 49.1 us -> none  [the longest x1 16.1 us: body(): lax.all_to_all(enc_send, 'seq', split_axis=0, concat_axis=0, tiled=True)]
    scatter x10 -> x0, local copies, waits for them, and re-layouts: 35.1 us -> none  [the longest x1 6.83 us: body(): enc_send = jnp.zeros((capacity, width), jnp.bfloat16).at[slot].set(encode...]
    unnamed x1 -> x0, blocking collectives: 26 us -> none
    reduce_sum x33 -> x0, other arithmetic: 24 us -> none  [the longest x16 11.7 us: head_attend(): probs = (expon / jnp.sum(expon, axis=1, keepdims=True)).astype(jnp.bfloat16)]
  transfers between devices with their start and end apart: 9 -> 0, of which waited for: 3 -> 0; matrix products, arithmetic and copies ran while one was open for 12% -> 0% of each run, Pallas kernels for 0% -> 0%
where the time goes in v1:
time: 107 us
  Pallas kernels  102 us (95%)
  local copies, waits for them, and re-layouts  4.52 us (4%)
    pallas_call x1, Pallas kernels, body(): pl.pallas_call(kernel, out_shape=(shape((1, ROWS, WIDTH), F32), shape((WI...  102 us
    unnamed x13, local copies, waits for them, and re-layouts  4.52 us

profile of v1, /device:TPU:1, one launch (start us, length us, event | category | flops | bytes accessed | tf_op | source)
XLA Modules:
  0.0 106.7 jit_solution(15531437518129557660)
XLA Ops:
  0.6 101.5 %shard_map.110 = (f32[1,1024,128]{2,1,0:T(8,128)}, f32[128,384]{1,0:T(8,128)}, f32[128,128]{1,0:T(8,128)}, f32[1,128]{1,0:T(1,128)}, f32[7,128]{1,0:T(8,128)}) custom-call(bf16[1,1024,128]{2,1,0:T(8,128)(2,1)} %pts_ref.1, bf16[1,1024,128]{2,1,0:T(8,128)(2,1)} %cot_ref.1, s32[1,1024]{1,0:T(1,128)} %order_ref.1, bf16[128,384]{1,0:T(8,128)(2,1)} %wqkv_ref.1, ...), custom_call_target="tpu_custom_call" | custom-call | tf_op jit(solution)/shard_map/pallas_call | solution.py:381
  102.2 0.0 copy-start
  102.2 1.9 %copy.17 = f32[1,1024,128]{2,1,0:T(8,128)} copy(f32[1,1024,128]{2,1,0:T(8,128)} %get-tuple-element.20) | data formatting | bytes 1048576
  104.1 0.0 copy-done
  104.1 0.0 copy-start.1
  104.1 0.7 copy.18
  104.8 0.2 copy-done.1
  104.9 0.0 copy-start.3
  104.9 0.0 copy-start.2
  104.9 0.6 copy.19
  105.6 0.0 copy-done.3
  105.6 0.5 copy.20
  106.1 0.0 copy-done.2
  106.1 0.6 copy.21
Async XLA Ops:
  102.2 1.9 %copy-start = (f32[128,384]{1,0:T(8,128)S(1)}, f32[128,384]{1,0:T(8,128)}, u32[]{:S(2)}) copy-start(f32[128,384]{1,0:T(8,128)} %get-tuple-element.21) | copy-start | bytes 589828
  104.1 0.9 copy-start.1
  104.9 0.6 copy-start.3
  104.9 1.1 %copy-start.2 = (f32[7,128]{1,0:T(8,128)S(1)}, f32[7,128]{1,0:T(8,128)}, u32[]{:S(2)}) copy-start(f32[7,128]{1,0:T(8,128)} %get-tuple-element.24) | copy-start | bytes 10756

commit v2 on v1

--- a/solution.py
+++ b/solution.py
@@ -39,10 +39,11 @@
 
 def kernel(
     pts_ref, cot_ref, order_ref, wqkv_ref, wout_ref, gain_ref, taps_ref,
-    gp_ref, gq_ref, gw_ref, gg_ref, gt_ref,
+    curve_ref, sums_ref, small_ref,
     pp, pb, pbt, pret, q4, mine, agz, agw, scot, senc,
-    tx, rx, bt, rr, patch, cotp,
+    tx, rx, c0, c1, c2, bt, rr, patch, cotp,
     qT, kT, vT, doT, kf, vf, attT, dqT, dkT, dvT, xhT, rs, nbT, sbuf, eb, xb, w1, mref,
+    oT, keT, invs,
     cpad, acc, rsb, part, zb, full, fin, tmine, tw, tsum, tz,
     ssem, rsem,
 ):
@@ -97,7 +98,8 @@
         pl.semaphore_signal(barrier, inc=1, device_id=dev, device_id_type=MESH)
 
     loop(NZ - 1, lambda t: greet(z_peer(t)[1]))
-    loop(NW - 1, lambda t: greet(w_peer(t)[1]))
+    loop(NYC - 1, lambda t: greet(yc_peer(t)[1]))
+    loop(NX - 1, lambda t: greet((me, lax.rem(rep + 1 + t, NX))))
     greet(nxt)
     greet(prv)
 
@@ -128,7 +130,7 @@
         [wq[:, j * WIDTH : (j + 1) * WIDTH].astype(F32).T.astype(BF) for j in range(3)], axis=0
     )
 
-    pl.semaphore_wait(barrier, NZ - 1 + NW - 1 + 2)
+    pl.semaphore_wait(barrier, NZ - 1 + NYC - 1 + NX - 1 + 2)
 
     def send_z(t):
         push(mine, agz.at[z], 0, z_peer(t)[1])
@@ -137,13 +139,6 @@
     push(pp.at[pl.ds(ROWS, 8)], pp.at[pl.ds(0, 8)], 1, nxt)
     push(pp.at[pl.ds(8, 8)], pp.at[pl.ds(ROWS + 8, 8)], 2, prv)
     agz[z] = mine[...]
-    wait_in(agz.at[pl.ds(0, NZ - 1)], 0)
-
-    def send_yc(t):
-        push(agz, agw.at[yc], 3, yc_peer(t)[1])
-
-    loop(NYC - 1, send_yc)
-    agw[yc] = agz[...]
     wait_in(pp.at[pl.ds(0, 8)], 1)
     wait_in(pp.at[pl.ds(ROWS + 8, 8)], 2)
     has_prev = jnp.where(me > 0, 1.0, 0.0)
@@ -156,6 +151,13 @@
     for t in range(7):
         enc = enc + taps_ref[t : t + 1, :] * pp[5 + t : 5 + t + ROWS, :]
     senc[...] = dot(pb[...], enc.astype(BF)).astype(BF)
+    wait_in(agz.at[pl.ds(0, NZ - 1)], 0)
+
+    def send_yc(t):
+        push(agz, agw.at[yc], 3, yc_peer(t)[1])
+
+    loop(NYC - 1, send_yc)
+    agw[yc] = agz[...]
     wait_in(agw.at[pl.ds(0, NYC - 1)], 3)
     owners = agw[...].reshape(SEQ, WIDTH)
     pick = hot(owners == iota((SEQ, WIDTH), 1).astype(F32))
@@ -163,8 +165,7 @@
     wide = ntdot(dot(grow, pick).astype(BF), grow)
     same = (iota((HALF, HALF), 0) % 4) == (iota((HALF, HALF), 1) % 4)
     q4[...] = jnp.where(same, wide, 0.0).astype(BF)
-    tx[:, 0:4, :] = dot(q4[...], senc[0:HALF, :]).astype(BF).reshape(SEQ, 4, WIDTH)
-    tx[:, 4:8, :] = dot(q4[...], scot[0:HALF, :]).astype(BF).reshape(SEQ, 4, WIDTH)
+    tx[...] = dot(q4[...], senc[0:HALF, :]).astype(BF).reshape(SEQ, 4, WIDTH)
 
     def send_rows(t):
         slot_of, dev = seq_peer(t)
@@ -172,14 +173,29 @@
 
     loop(SEQ - 1, send_rows)
     rx[sig] = tx[sig]
+    c0[...] = dot(q4[...], scot[0:HALF, :]).astype(BF).reshape(NYC, NZ, 4, WIDTH)
+
+    def send_cot(t):
+        cc, dev = yc_peer(t)
+        push(c0.at[cc], c1.at[yc], 13, dev)
+
+    loop(NYC - 1, send_cot)
+    c1[yc] = c0[yc]
     pret[...] = ntdot(pbt[:, 0:HALF], q4[...]).astype(BF)
     patch[HALF:, :] = senc[HALF:, :]
     cotp[HALF:, :] = scot[HALF:, :]
     gain = gain_ref[...]
     gainc = jnp.sum(jnp.where(eye.astype(F32) > 0.5, gain, 0.0), axis=1, keepdims=True)
+    wait_in(c1.at[pl.ds(0, NYC - 1)], 13)
     wait_in(rx.at[pl.ds(0, SEQ - 1)], 4)
-    patch[0:HALF, :] = rx[:, 0:4, :].reshape(HALF, WIDTH)
-    cotp[0:HALF, :] = rx[:, 4:8, :].reshape(HALF, WIDTH)
+
+    def send_cot_z(t):
+        zz, dev = z_peer(t)
+        push(c1.at[:, zz], c2.at[:, z], 14, dev)
+
+    loop(NZ - 1, send_cot_z)
+    c2[:, z] = c1[:, z]
+    patch[0:HALF, :] = rx[...].reshape(HALF, WIDTH)
 
     xT = ntdot(eye, patch[...])
     center = xT - jnp.mean(xT, axis=0, keepdims=True)
@@ -196,7 +212,6 @@
     vT[...] = qkvT[256:384]
     kf[...] = mixed[128:256].T.astype(BF)
     vf[...] = mixed[256:384].T.astype(BF)
-    doT[...] = ntdot(wout_ref[...], cotp[...]).astype(BF)
     ones = jnp.ones((16, ROWS), BF)
     for h in range(HEADS):
         w1[h * 48 : h * 48 + 16, :] = qkvT[256 + h * 16 : 272 + h * 16]
@@ -211,11 +226,10 @@
     sbuf[0] = first
     mref[0] = jnp.broadcast_to(jnp.max(first, axis=0, keepdims=True), (8, ROWS))
 
-    def head(h, cur, other, last):
+    def forward(h, cur, other, last):
         hs = pl.ds(pl.multiple_of(h * 16, 16), 16)
         if not last:
             q_next = masked(qT, h + 1)
-        do_wide = masked(doT, h)
         top = mref[cur][0:1, :]
         top_next = None
         for c in range(4):
@@ -225,34 +239,53 @@
                 sbuf[other, ks, :] = s
                 high = jnp.max(s, axis=0, keepdims=True)
                 top_next = high if top_next is None else jnp.maximum(top_next, high)
-            e = jnp.exp(sbuf[cur, ks, :] - top)
-            t = dot(vf[ks, :], do_wide)
-            eb[ks, :] = e.astype(BF)
-            xb[ks, :] = (e * t).astype(BF)
+            eb[h, ks, :] = jnp.exp(sbuf[cur, ks, :] - top).astype(BF)
         if not last:
             mref[other] = jnp.broadcast_to(top_next, (8, ROWS))
-        a = dot(w1[pl.ds(pl.multiple_of(h * 48, 16), 48), :], eb[...])
+        a = dot(w1[pl.ds(pl.multiple_of(h * 48, 16), 48), :], eb[h])
         inv = 1.0 / a[16:17]
         o = a[0:16] * inv
         attT[hs, :] = o.astype(BF)
-        kx = dot(kT[hs, :], xb[...])
+        oT[hs, :] = o
+        keT[hs, :] = a[32:48]
+        invs[h] = jnp.broadcast_to(inv, (8, ROWS))
+
+    def backward(h):
+        hs = pl.ds(pl.multiple_of(h * 16, 16), 16)
+        do_wide = masked(doT, h)
+        for c in range(4):
+            ks = slice(c * 256, c * 256 + 256)
+            t = dot(vf[ks, :], do_wide)
+            xb[ks, :] = (eb[h, ks, :].astype(F32) * t).astype(BF)
+        inv = invs[h][0:1, :]
         do = doT[hs, :].astype(F32)
         q = qT[hs, :].astype(F32)
-        delta = jnp.sum(do * o, axis=0, keepdims=True)
-        dqT[hs, :] = ((kx - delta * a[32:48]) * (inv * 0.25)).astype(BF)
-        back = ntdot(jnp.concatenate([do * inv, q * (-delta * inv)], axis=0).astype(BF), eb[...])
+        delta = jnp.sum(do * oT[hs, :], axis=0, keepdims=True)
+        back = ntdot(jnp.concatenate([do * inv, q * (-delta * inv)], axis=0).astype(BF), eb[h])
+        kx = dot(kT[hs, :], xb[...])
+        dqT[hs, :] = ((kx - delta * keT[hs, :]) * (inv * 0.25)).astype(BF)
         dk = ntdot((q * inv).astype(BF), xb[...])
         dvT[hs, :] = back[0:16].astype(BF)
         dkT[hs, :] = (dk + back[16:32]).astype(BF)
 
     def pair(i, carry):
-        head(2 * i, 0, 1, False)
-        head(2 * i + 1, 1, 0, False)
+        forward(2 * i, 0, 1, False)
+        forward(2 * i + 1, 1, 0, False)
         return carry
 
     lax.fori_loop(0, HEADS // 2 - 1, pair, 0)
-    head(HEADS - 2, 0, 1, False)
-    head(HEADS - 1, 1, 0, True)
+    forward(HEADS - 2, 0, 1, False)
+    forward(HEADS - 1, 1, 0, True)
+
+    wait_in(c2.at[:, pl.ds(0, NZ - 1)], 14)
+    cotp[0:HALF, :] = c2[...].reshape(HALF, WIDTH)
+    doT[...] = ntdot(wout_ref[...], cotp[...]).astype(BF)
+
+    def back_head(h, carry):
+        backward(h)
+        return carry
+
+    lax.fori_loop(0, HEADS, back_head, 0)
 
     dall = jnp.concatenate([dqT[...], dkT[...], dvT[...]], axis=0)
     dnT = dot(wq, dall).astype(BF).astype(F32)
@@ -264,26 +297,25 @@
     patch[...] = (dxT.T + cotp[...].astype(F32)).astype(BF)
     bt[...] = patch[0:HALF, :].reshape(SEQ, 4, WIDTH)
 
+    for j in range(3):
+        acc[j * 8 : j * 8 + 8] = ntdot(nbT[...], dall[j * WIDTH : (j + 1) * WIDTH]).reshape(8, 16, WIDTH)
+    acc[24:32] = dot(attT[...], cotp[...]).reshape(8, 16, WIDTH)
+
+    def send_part(t):
+        ww, dev = w_peer(t)
+        push(acc.at[ww], rsb.at[w], 6, dev)
+
+    loop(NW - 1, send_part)
+    rsb[w] = acc[w]
+
     def send_back(t):
         slot_of, dev = seq_peer(t)
         push(bt.at[slot_of], rr.at[sig], 5, dev)
 
     loop(SEQ - 1, send_back)
     rr[sig] = bt[sig]
-
     ggT = jnp.sum(dnT * xh, axis=1, keepdims=True)
     gain_row = jnp.sum(jnp.where(eye.astype(F32) > 0.5, ggT, 0.0), axis=0, keepdims=True)
-    for j in range(3):
-        acc[j * 8 : j * 8 + 8] = ntdot(nbT[...], dall[j * WIDTH : (j + 1) * WIDTH]).reshape(8, 16, WIDTH)
-    acc[24:32] = dot(attT[...], cotp[...]).reshape(8, 16, WIDTH)
-
-    def send_part(t):
-        ww, dev = w_peer(t)
-        push(acc.at[ww], rsb.at[w], 6, dev)
-
-    loop(NW - 1, send_part)
-    rsb[w] = acc[w]
-    own = dot(pbt[:, HALF:], patch[HALF:, :])
     wait_in(rsb.at[pl.ds(0, NW - 1)], 6)
     part[...] = jnp.sum(rsb[...], axis=0)
 
@@ -292,6 +324,7 @@
 
     loop(NZ - 1, send_part_z)
     zb[z] = part[...]
+    own = dot(pbt[:, HALF:], patch[HALF:, :])
 
     wait_in(rr.at[pl.ds(0, SEQ - 1)], 5)
     cb = own + dot(pret[...], rr[...].reshape(HALF, WIDTH))
@@ -306,6 +339,16 @@
 
     loop(NW - 1, send_tap)
     tw[w] = tmine[...]
+    curve_ref[16 : 16 + ROWS, :] = cb.astype(BF)
+
+    wait_in(tw.at[pl.ds(0, NW - 1)], 10)
+    tsum[...] = jnp.sum(tw[...], axis=0)
+
+    def send_tap_z(t):
+        push(tsum, tz.at[z], 12, z_peer(t)[1])
+
+    loop(NZ - 1, send_tap_z)
+    tz[z] = tsum[...]
 
     wait_in(zb.at[pl.ds(0, NZ - 1)], 7)
     full[...] = jnp.sum(zb[...], axis=0)
@@ -315,39 +358,22 @@
 
     loop(NW - 1, send_full)
     fin[w] = full[...]
-
-    wait_in(tw.at[pl.ds(0, NW - 1)], 10)
-    tsum[...] = jnp.sum(tw[...], axis=0)
-
-    def send_tap_z(t):
-        push(tsum, tz.at[z], 12, z_peer(t)[1])
-
-    loop(NZ - 1, send_tap_z)
-    tz[z] = tsum[...]
 
     wait_in(cpad.at[pl.ds(0, 8)], 8)
     wait_in(cpad.at[pl.ds(ROWS + 8, 8)], 9)
     wait_out(cpad.at[pl.ds(ROWS, 8)], 8)
     wait_out(cpad.at[pl.ds(8, 8)], 9)
-    cpad[0:8, :] = cpad[0:8, :] * has_prev
-    cpad[ROWS + 8 : ROWS + 16, :] = cpad[ROWS + 8 : ROWS + 16, :] * has_next
-    res = cpad[8 : 8 + ROWS, :]
-    for t in range(7):
-        res = res + taps_ref[t : t + 1, :] * cpad[11 - t : 11 - t + ROWS, :]
-    gp_ref[0] = res
-
-    wait_in(fin.at[pl.ds(0, NW - 1)], 11)
-    for j in range(3):
-        gq_ref[:, j * WIDTH : (j + 1) * WIDTH] = fin[j * 8 : j * 8 + 8].reshape(WIDTH, WIDTH)
-    gw_ref[...] = fin[24:32].reshape(WIDTH, WIDTH)
-    wait_in(tz.at[pl.ds(0, NZ - 1)], 12)
-    total = jnp.sum(tz[...], axis=0)
-    gt_ref[...] = total[0:7]
-    gg_ref[...] = total[7:8]
+    zero = jnp.zeros((8, WIDTH), F32)
+    curve_ref[0:16, :] = jnp.concatenate([zero, cpad[0:8, :] * has_prev], axis=0).astype(BF)
+    curve_ref[ROWS + 16 : ROWS + 32, :] = jnp.concatenate(
+        [cpad[ROWS + 8 : ROWS + 16, :] * has_next, zero], axis=0
+    ).astype(BF)
 
     wait_out(agz.at[pl.ds(0, NZ - 1)], 0)
     wait_out(agw.at[pl.ds(0, NYC - 1)], 3)
     wait_out(rx.at[pl.ds(0, SEQ - 1)], 4)
+    wait_out(c1.at[pl.ds(0, NYC - 1)], 13)
+    wait_out(c2.at[:, pl.ds(0, NZ - 1)], 14)
     wait_out(rr.at[pl.ds(0, SEQ - 1)], 5)
     wait_out(rsb.at[pl.ds(0, NW - 1)], 6)
     wait_out(zb.at[pl.ds(0, NZ - 1)], 7)
@@ -355,6 +381,24 @@
     wait_out(fin.at[pl.ds(0, NW - 1)], 11)
     wait_out(tz.at[pl.ds(0, NZ - 1)], 12)
 
+    wait_in(fin.at[pl.ds(0, NW - 1)], 11)
+    sums_ref[...] = fin[...].reshape(HALF, WIDTH)
+    wait_in(tz.at[pl.ds(0, NZ - 1)], 12)
+    small_ref[...] = jnp.sum(tz[...], axis=0)
+
+
+def finish(curve_ref, sums_ref, small_ref, taps_ref, gp_ref, gq_ref, gw_ref, gg_ref, gt_ref, cpad):
+    cpad[...] = curve_ref[...].astype(F32)
+    res = cpad[16 : 16 + ROWS, :]
+    for t in range(7):
+        res = res + taps_ref[t : t + 1, :] * cpad[19 - t : 19 - t + ROWS, :]
+    gp_ref[0] = res
+    for j in range(3):
+        gq_ref[:, j * WIDTH : (j + 1) * WIDTH] = sums_ref[j * WIDTH : (j + 1) * WIDTH, :]
+    gw_ref[...] = sums_ref[3 * WIDTH :, :]
+    gt_ref[...] = small_ref[0:7, :]
+    gg_ref[...] = small_ref[7:8, :]
+
 
 def body(points, grad_rows, order, w_qkv, w_out, norm_gain, conv_taps):
     def vm(shape, dtype):
@@ -366,31 +410,41 @@
     scratch = [
         vm((ROWS + 16, WIDTH), F32), vm(sq, BF), vm(sq, BF), vm((ROWS, HALF), BF), vm((HALF, HALF), BF),
         vm((1, WIDTH), F32), vm((NZ, 1, WIDTH), F32), vm((NYC, NZ, 1, WIDTH), F32), vm(tall, BF), vm(tall, BF),
-        vm((SEQ, 8, WIDTH), BF), vm((SEQ, 8, WIDTH), BF), vm((SEQ, 4, WIDTH), BF), vm((SEQ, 4, WIDTH), BF),
+        vm((SEQ, 4, WIDTH), BF), vm((SEQ, 4, WIDTH), BF),
+        vm((NYC, NZ, 4, WIDTH), BF), vm((NYC, NZ, 4, WIDTH), BF), vm((NYC, NZ, 4, WIDTH), BF),
+        vm((SEQ, 4, WIDTH), BF), vm((SEQ, 4, WIDTH), BF),
         vm(tall, BF), vm(tall, BF),
         vm(wide, BF), vm(wide, BF), vm(wide, BF), vm(wide, BF), vm(tall, BF), vm(tall, BF),
         vm(wide, BF), vm(wide, BF), vm(wide, BF), vm(wide, BF), vm(wide, F32), vm((8, ROWS), F32), vm(wide, BF),
-        vm((2,) + sq, F32), vm(sq, BF), vm(sq, BF), vm((HEADS * 48, ROWS), BF), vm((2, 8, ROWS), F32),
+        vm((2,) + sq, F32), vm((HEADS,) + sq, BF), vm(sq, BF), vm((HEADS * 48, ROWS), BF), vm((2, 8, ROWS), F32),
+        vm(wide, F32), vm(wide, F32), vm((HEADS, 8, ROWS), F32),
         vm((ROWS + 16, WIDTH), F32), vm((NW, 16, WIDTH), F32), vm((NW, 16, WIDTH), F32), vm((16, WIDTH), F32),
         vm((NZ, 16, WIDTH), F32), vm((16, WIDTH), F32), vm((NW, 16, WIDTH), F32),
         vm((8, WIDTH), F32), vm((NW, 8, WIDTH), F32), vm((8, WIDTH), F32), vm((NZ, 8, WIDTH), F32),
-        pltpu.SemaphoreType.DMA((13,)), pltpu.SemaphoreType.DMA((13,)),
+        pltpu.SemaphoreType.DMA((15,)), pltpu.SemaphoreType.DMA((15,)),
     ]
     spec = pl.BlockSpec(memory_space=pltpu.VMEM)
     shape = jax.ShapeDtypeStruct
-    gp, gq, gw, gg, gt = pl.pallas_call(
+    curve, sums, small = pl.pallas_call(
         kernel,
-        out_shape=(
-            shape((1, ROWS, WIDTH), F32), shape((WIDTH, 3 * WIDTH), F32), shape((WIDTH, WIDTH), F32),
-            shape((1, WIDTH), F32), shape((7, WIDTH), F32),
-        ),
+        out_shape=(shape((ROWS + 32, WIDTH), BF), shape((HALF, WIDTH), F32), shape((8, WIDTH), F32)),
         in_specs=[spec] * 7,
-        out_specs=[spec] * 5,
+        out_specs=[spec] * 3,
         scratch_shapes=scratch,
         compiler_params=pltpu.CompilerParams(
             collective_id=0, has_side_effects=True, vmem_limit_bytes=56 * 2**20
         ),
     )(points, grad_rows, order, w_qkv, w_out, norm_gain.reshape(1, WIDTH), conv_taps)
+    gp, gq, gw, gg, gt = pl.pallas_call(
+        finish,
+        out_shape=(
+            shape((1, ROWS, WIDTH), F32), shape((WIDTH, 3 * WIDTH), F32), shape((WIDTH, WIDTH), F32),
+            shape((1, WIDTH), F32), shape((7, WIDTH), F32),
+        ),
+        in_specs=[spec] * 4,
+        out_specs=[spec] * 5,
+        scratch_shapes=[vm((ROWS + 32, WIDTH), F32)],
+    )(curve, sums, small, conv_taps)
     return gp, gq, gw, gg.reshape(WIDTH), gt
 
 

time: 107 us -> 103 us (0.963)
  local copies, waits for them, and re-layouts: 4.52 us -> 0 us
    unnamed x13 -> x0, local copies, waits for them, and re-layouts: 4.52 us -> none
    pallas_call x1 -> x2, Pallas kernels: 102 us -> 103 us  [the longest x1 100 us: body(): pl.pallas_call(kernel, out_shape=(shape((ROWS + 32, WIDTH), BF), shape((H...]
where the time goes in v2:
time: 103 us
  Pallas kernels  103 us (100%)
    pallas_call x1, Pallas kernels, body(): pl.pallas_call(kernel, out_shape=(shape((ROWS + 32, WIDTH), BF), shape((H...  100 us
    pallas_call x1, Pallas kernels, body(): pl.pallas_call(finish, out_shape=(shape((1, ROWS, WIDTH), F32), shape((WI...  2.41 us

profile of v2, /device:TPU:1, one launch (start us, length us, event | category | flops | bytes accessed | tf_op | source)
XLA Modules:
  0.0 103.3 jit_solution(3070917535315897373)
XLA Ops:
  0.6 100.2 %shard_map.110 = (bf16[1056,128]{1,0:T(8,128)(2,1)}, f32[512,128]{1,0:T(8,128)}, f32[8,128]{1,0:T(8,128)}) custom-call(bf16[1,1024,128]{2,1,0:T(8,128)(2,1)} %pts_ref.1, bf16[1,1024,128]{2,1,0:T(8,128)(2,1)} %cot_ref.1, s32[1,1024]{1,0:T(1,128)} %order_ref.1, bf16[128,384]{1,0:T(8,128)(2,1)} %wqkv_ref.1, bf16[128,128]{1,0:T(8,128)(2,1)} %wout_ref.1, ...), custom_call_target="tpu_custom_call" | custom-call | tf_op jit(solution)/shard_map/pallas_call | solution.py:428
  100.9 2.4 %shard_map.111 = (f32[1,1024,128]{2,1,0:T(8,128)}, f32[128,384]{1,0:T(8,128)}, f32[128,128]{1,0:T(8,128)}, f32[1,128]{1,0:T(1,128)}, f32[7,128]{1,0:T(8,128)}) custom-call(bf16[1056,128]{1,0:T(8,128)(2,1)} %get-tuple-element.13.curve_ref, f32[512,128]{1,0:T(8,128)} %get-tuple-element.14.sums_ref, f32[8,128]{1,0:T(8,128)} %get-tuple-element.15.small_ref, ...), custom_call_target="tpu_custom_call" | custom-call | tf_op jit(solution)/shard_map/pallas_call | solution.py:438

commit v3 on v2

--- a/solution.py
+++ b/solution.py
@@ -40,7 +40,7 @@
 def kernel(
     pts_ref, cot_ref, order_ref, wqkv_ref, wout_ref, gain_ref, taps_ref,
     curve_ref, sums_ref, small_ref,
-    pp, pb, pbt, pret, q4, mine, agz, agw, scot, senc,
+    pp, pown, pret, q4, mine, agz, agw, scot, senc,
     tx, rx, c0, c1, c2, bt, rr, patch, cotp,
     qT, kT, vT, doT, kf, vf, attT, dqT, dkT, dvT, xhT, rs, nbT, sbuf, eb, xb, w1, mref,
     oT, keT, invs,
@@ -93,6 +93,8 @@
         pltpu.make_async_copy(ref, ref, ssem.at[k]).wait()
 
     barrier = pltpu.get_barrier_semaphore()
+    pb = xb.at[0]
+    pbt = xb.at[1]
 
     def greet(dev):
         pl.semaphore_signal(barrier, inc=1, device_id=dev, device_id_type=MESH)
@@ -123,6 +125,7 @@
     pb[...] = hot(iota((ROWS, ROWS), 0).astype(F32) == slot)
     slot_col = jnp.broadcast_to(slot, (8, ROWS)).T[:, 0:1]
     pbt[...] = hot(iota((ROWS, ROWS), 1).astype(F32) == slot_col)
+    pown[...] = pbt[:, HALF:]
     scot[...] = dot(pb[...], cot_ref[0]).astype(BF)
     eye = hot(iota((WIDTH, WIDTH), 0) == iota((WIDTH, WIDTH), 1))
     wq = wqkv_ref[...]
@@ -226,23 +229,11 @@
     sbuf[0] = first
     mref[0] = jnp.broadcast_to(jnp.max(first, axis=0, keepdims=True), (8, ROWS))
 
-    def forward(h, cur, other, last):
+    def weighted(h, ks):
+        return dot(w1[pl.ds(pl.multiple_of(h * 48, 16), 48), ks], eb[h, ks, :])
+
+    def close(h, a):
         hs = pl.ds(pl.multiple_of(h * 16, 16), 16)
-        if not last:
-            q_next = masked(qT, h + 1)
-        top = mref[cur][0:1, :]
-        top_next = None
-        for c in range(4):
-            ks = slice(c * 256, c * 256 + 256)
-            if not last:
-                s = dot(kf[ks, :], q_next)
-                sbuf[other, ks, :] = s
-                high = jnp.max(s, axis=0, keepdims=True)
-                top_next = high if top_next is None else jnp.maximum(top_next, high)
-            eb[h, ks, :] = jnp.exp(sbuf[cur, ks, :] - top).astype(BF)
-        if not last:
-            mref[other] = jnp.broadcast_to(top_next, (8, ROWS))
-        a = dot(w1[pl.ds(pl.multiple_of(h * 48, 16), 48), :], eb[h])
         inv = 1.0 / a[16:17]
         o = a[0:16] * inv
         attT[hs, :] = o.astype(BF)
@@ -250,55 +241,98 @@
         keT[hs, :] = a[32:48]
         invs[h] = jnp.broadcast_to(inv, (8, ROWS))
 
-    def backward(h):
+    def forward(h, cur, first, last):
+        if not last:
+            q_next = masked(qT, h + 1)
+        top = mref[cur][0:1, :]
+        top_next = None
+        a = None
+        for c in range(4):
+            ks = slice(c * 256, c * 256 + 256)
+            if not last:
+                s = dot(kf[ks, :], q_next)
+                sbuf[1 - cur, ks, :] = s
+                high = jnp.max(s, axis=0, keepdims=True)
+                top_next = high if top_next is None else jnp.maximum(top_next, high)
+            eb[h, ks, :] = jnp.exp(sbuf[cur, ks, :] - top).astype(BF)
+            if not first:
+                part_a = weighted(h - 1, ks)
+                a = part_a if a is None else a + part_a
+        if not last:
+            mref[1 - cur] = jnp.broadcast_to(top_next, (8, ROWS))
+        if not first:
+            close(h - 1, a)
+
+    def pair(i, carry):
+        forward(2 * i + 1, 1, False, False)
+        forward(2 * i + 2, 0, False, False)
+        return carry
+
+    forward(0, 0, True, False)
+    lax.fori_loop(0, HEADS // 2 - 1, pair, 0)
+    forward(HEADS - 1, 1, False, True)
+    close(HEADS - 1, weighted(HEADS - 1, slice(0, ROWS)))
+
+    wait_in(c2.at[:, pl.ds(0, NZ - 1)], 14)
+    cotp[0:HALF, :] = c2[...].reshape(HALF, WIDTH)
+    doT[...] = ntdot(wout_ref[...], cotp[...]).astype(BF)
+
+    def backward(h, cols):
         hs = pl.ds(pl.multiple_of(h * 16, 16), 16)
+        inv = invs[h][0:1, :]
+        do = doT[hs, :].astype(F32)
+        q = qT[hs, :].astype(F32)
+        delta = jnp.sum(do * oT[hs, :], axis=0, keepdims=True)
+        lead = jnp.concatenate([do * inv, q * (-delta * inv)], axis=0).astype(BF)
+        back = ntdot(lead, eb[h, cols, :])
+        kx = dot(kT[hs, :], xb[h, :, cols])
+        dqT[hs, cols] = ((kx - delta[:, cols] * keT[hs, cols]) * (inv[:, cols] * 0.25)).astype(BF)
+        dk = ntdot((q * inv).astype(BF), xb[h, cols, :])
+        dvT[hs, cols] = back[0:16].astype(BF)
+        dkT[hs, cols] = (dk + back[16:32]).astype(BF)
+
+    def input_grads(cols):
+        dall = jnp.concatenate([dqT[:, cols], dkT[:, cols], dvT[:, cols]], axis=0)
+        dnT = dot(wq, dall).astype(BF).astype(F32)
+        xh = xhT[:, cols]
+        dxh = dnT * gainc
+        m1 = jnp.mean(dxh, axis=0, keepdims=True)
+        m2 = jnp.mean(dxh * xh, axis=0, keepdims=True)
+        dxT = (dxh - m1 - xh * m2) * rs[0:1, cols]
+        patch[cols, :] = (dxT.T + cotp[cols, :].astype(F32)).astype(BF)
+        return jnp.sum(dnT * xh, axis=1, keepdims=True)
+
+    sent = slice(0, HALF)
+    kept = slice(HALF, ROWS)
+
+    def back_sent(h, carry):
         do_wide = masked(doT, h)
         for c in range(4):
             ks = slice(c * 256, c * 256 + 256)
             t = dot(vf[ks, :], do_wide)
-            xb[ks, :] = (eb[h, ks, :].astype(F32) * t).astype(BF)
-        inv = invs[h][0:1, :]
-        do = doT[hs, :].astype(F32)
-        q = qT[hs, :].astype(F32)
-        delta = jnp.sum(do * oT[hs, :], axis=0, keepdims=True)
-        back = ntdot(jnp.concatenate([do * inv, q * (-delta * inv)], axis=0).astype(BF), eb[h])
-        kx = dot(kT[hs, :], xb[...])
-        dqT[hs, :] = ((kx - delta * keT[hs, :]) * (inv * 0.25)).astype(BF)
-        dk = ntdot((q * inv).astype(BF), xb[...])
-        dvT[hs, :] = back[0:16].astype(BF)
-        dkT[hs, :] = (dk + back[16:32]).astype(BF)
-
-    def pair(i, carry):
-        forward(2 * i, 0, 1, False)
-        forward(2 * i + 1, 1, 0, False)
+            xb[h, ks, :] = (eb[h, ks, :].astype(F32) * t).astype(BF)
+        backward(h, sent)
         return carry
 
-    lax.fori_loop(0, HEADS // 2 - 1, pair, 0)
-    forward(HEADS - 2, 0, 1, False)
-    forward(HEADS - 1, 1, 0, True)
-
-    wait_in(c2.at[:, pl.ds(0, NZ - 1)], 14)
-    cotp[0:HALF, :] = c2[...].reshape(HALF, WIDTH)
-    doT[...] = ntdot(wout_ref[...], cotp[...]).astype(BF)
-
-    def back_head(h, carry):
-        backward(h)
+    def back_kept(h, carry):
+        backward(h, kept)
         return carry
 
-    lax.fori_loop(0, HEADS, back_head, 0)
-
-    dall = jnp.concatenate([dqT[...], dkT[...], dvT[...]], axis=0)
-    dnT = dot(wq, dall).astype(BF).astype(F32)
-    xh = xhT[...]
-    dxh = dnT * gainc
-    m1 = jnp.mean(dxh, axis=0, keepdims=True)
-    m2 = jnp.mean(dxh * xh, axis=0, keepdims=True)
-    dxT = (dxh - m1 - xh * m2) * rs[0:1, :]
-    patch[...] = (dxT.T + cotp[...].astype(F32)).astype(BF)
-    bt[...] = patch[0:HALF, :].reshape(SEQ, 4, WIDTH)
-
-    for j in range(3):
-        acc[j * 8 : j * 8 + 8] = ntdot(nbT[...], dall[j * WIDTH : (j + 1) * WIDTH]).reshape(8, 16, WIDTH)
+    lax.fori_loop(0, HEADS, back_sent, 0)
+    ggT = input_grads(sent)
+    bt[...] = patch[sent, :].reshape(SEQ, 4, WIDTH)
+
+    def send_back(t):
+        slot_of, dev = seq_peer(t)
+        push(bt.at[slot_of], rr.at[sig], 5, dev)
+
+    loop(SEQ - 1, send_back)
+    rr[sig] = bt[sig]
+    lax.fori_loop(0, HEADS, back_kept, 0)
+    ggT = ggT + input_grads(kept)
+
+    for j, grad in enumerate((dqT, dkT, dvT)):
+        acc[j * 8 : j * 8 + 8] = ntdot(nbT[...], grad[...]).reshape(8, 16, WIDTH)
     acc[24:32] = dot(attT[...], cotp[...]).reshape(8, 16, WIDTH)
 
     def send_part(t):
@@ -307,14 +341,6 @@
 
     loop(NW - 1, send_part)
     rsb[w] = acc[w]
-
-    def send_back(t):
-        slot_of, dev = seq_peer(t)
-        push(bt.at[slot_of], rr.at[sig], 5, dev)
-
-    loop(SEQ - 1, send_back)
-    rr[sig] = bt[sig]
-    ggT = jnp.sum(dnT * xh, axis=1, keepdims=True)
     gain_row = jnp.sum(jnp.where(eye.astype(F32) > 0.5, ggT, 0.0), axis=0, keepdims=True)
     wait_in(rsb.at[pl.ds(0, NW - 1)], 6)
     part[...] = jnp.sum(rsb[...], axis=0)
@@ -324,7 +350,7 @@
 
     loop(NZ - 1, send_part_z)
     zb[z] = part[...]
-    own = dot(pbt[:, HALF:], patch[HALF:, :])
+    own = dot(pown[...], patch[HALF:, :])
 
     wait_in(rr.at[pl.ds(0, SEQ - 1)], 5)
     cb = own + dot(pret[...], rr[...].reshape(HALF, WIDTH))
@@ -408,7 +434,7 @@
     wide = (WIDTH, ROWS)
     tall = (ROWS, WIDTH)
     scratch = [
-        vm((ROWS + 16, WIDTH), F32), vm(sq, BF), vm(sq, BF), vm((ROWS, HALF), BF), vm((HALF, HALF), BF),
+        vm((ROWS + 16, WIDTH), F32), vm((ROWS, HALF), BF), vm((ROWS, HALF), BF), vm((HALF, HALF), BF),
         vm((1, WIDTH), F32), vm((NZ, 1, WIDTH), F32), vm((NYC, NZ, 1, WIDTH), F32), vm(tall, BF), vm(tall, BF),
         vm((SEQ, 4, WIDTH), BF), vm((SEQ, 4, WIDTH), BF),
         vm((NYC, NZ, 4, WIDTH), BF), vm((NYC, NZ, 4, WIDTH), BF), vm((NYC, NZ, 4, WIDTH), BF),
@@ -416,7 +442,7 @@
         vm(tall, BF), vm(tall, BF),
         vm(wide, BF), vm(wide, BF), vm(wide, BF), vm(wide, BF), vm(tall, BF), vm(tall, BF),
         vm(wide, BF), vm(wide, BF), vm(wide, BF), vm(wide, BF), vm(wide, F32), vm((8, ROWS), F32), vm(wide, BF),
-        vm((2,) + sq, F32), vm((HEADS,) + sq, BF), vm(sq, BF), vm((HEADS * 48, ROWS), BF), vm((2, 8, ROWS), F32),
+        vm((2,) + sq, F32), vm((HEADS,) + sq, BF), vm((HEADS,) + sq, BF), vm((HEADS * 48, ROWS), BF), vm((2, 8, ROWS), F32),
         vm(wide, F32), vm(wide, F32), vm((HEADS, 8, ROWS), F32),
         vm((ROWS + 16, WIDTH), F32), vm((NW, 16, WIDTH), F32), vm((NW, 16, WIDTH), F32), vm((16, WIDTH), F32),
         vm((NZ, 16, WIDTH), F32), vm((16, WIDTH), F32), vm((NW, 16, WIDTH), F32),
@@ -432,7 +458,7 @@
         out_specs=[spec] * 3,
         scratch_shapes=scratch,
         compiler_params=pltpu.CompilerParams(
-            collective_id=0, has_side_effects=True, vmem_limit_bytes=56 * 2**20
+            collective_id=0, has_side_effects=True, vmem_limit_bytes=60 * 2**20
         ),
     )(points, grad_rows, order, w_qkv, w_out, norm_gain.reshape(1, WIDTH), conv_taps)
     gp, gq, gw, gg, gt = pl.pallas_call(

time: 103 us -> 99.7 us (0.968)
  Pallas kernels: 103 us -> 98.9 us
    pallas_call x1, Pallas kernels: 100 us -> 96.5 us  [body(): pl.pallas_call(kernel, out_shape=(shape((ROWS + 32, WIDTH), BF), shape((H...]
where the time goes in v3:
time: 99.7 us; the launch traced here: 99.5 us
  Pallas kernels  98.9 us (99%)
    pallas_call x1, Pallas kernels, body(): pl.pallas_call(kernel, out_shape=(shape((ROWS + 32, WIDTH), BF), shape((H...  96.5 us
    pallas_call x1, Pallas kernels, body(): pl.pallas_call(finish, out_shape=(shape((1, ROWS, WIDTH), F32), shape((WI...  2.41 us

profile of v3, /device:TPU:1, one launch (start us, length us, event | category | flops | bytes accessed | tf_op | source)
XLA Modules:
  0.0 99.5 jit_solution(3096167862018384010)
XLA Ops:
  0.6 96.5 %shard_map.110 = (bf16[1056,128]{1,0:T(8,128)(2,1)}, f32[512,128]{1,0:T(8,128)}, f32[8,128]{1,0:T(8,128)}) custom-call(bf16[1,1024,128]{2,1,0:T(8,128)(2,1)} %pts_ref.1, bf16[1,1024,128]{2,1,0:T(8,128)(2,1)} %cot_ref.1, s32[1,1024]{1,0:T(1,128)} %order_ref.1, bf16[128,384]{1,0:T(8,128)(2,1)} %wqkv_ref.1, bf16[128,128]{1,0:T(8,128)(2,1)} %wout_ref.1, ...), custom_call_target="tpu_custom_call" | custom-call | tf_op jit(solution)/shard_map/pallas_call | solution.py:454
  97.1 2.4 %shard_map.111 = (f32[1,1024,128]{2,1,0:T(8,128)}, f32[128,384]{1,0:T(8,128)}, f32[128,128]{1,0:T(8,128)}, f32[1,128]{1,0:T(1,128)}, f32[7,128]{1,0:T(8,128)}) custom-call(bf16[1056,128]{1,0:T(8,128)(2,1)} %get-tuple-element.13.curve_ref, f32[512,128]{1,0:T(8,128)} %get-tuple-element.14.sums_ref, f32[8,128]{1,0:T(8,128)} %get-tuple-element.15.small_ref, ...), custom_call_target="tpu_custom_call" | custom-call | tf_op jit(solution)/shard_map/pallas_call | solution.py:464

commit v4 on v3

--- a/solution.py
+++ b/solution.py
@@ -93,6 +93,8 @@
         pltpu.make_async_copy(ref, ref, ssem.at[k]).wait()
 
     barrier = pltpu.get_barrier_semaphore()
+    sent = slice(0, HALF)
+    kept = slice(HALF, ROWS)
     pb = xb.at[0]
     pbt = xb.at[1]
 
@@ -187,10 +189,31 @@
     pret[...] = ntdot(pbt[:, 0:HALF], q4[...]).astype(BF)
     patch[HALF:, :] = senc[HALF:, :]
     cotp[HALF:, :] = scot[HALF:, :]
+    def project(cols):
+        xT = ntdot(eye, patch[cols, :])
+        center = xT - jnp.mean(xT, axis=0, keepdims=True)
+        r = lax.rsqrt(jnp.mean(center * center, axis=0, keepdims=True) + 1e-5)
+        xh = center * r
+        xhT[:, cols] = xh
+        rs[:, cols] = jnp.broadcast_to(r, (8, HALF))
+        nT = (xh * gainc).astype(BF)
+        nbT[:, cols] = nT
+        mixed = dot(wqT, nT)
+        qkvT = mixed.astype(BF)
+        qT[:, cols] = qkvT[0:128] * jnp.asarray(0.25, BF)
+        kT[:, cols] = qkvT[128:256]
+        vT[:, cols] = qkvT[256:384]
+        kf[cols, :] = mixed[128:256].T.astype(BF)
+        vf[cols, :] = mixed[256:384].T.astype(BF)
+        for h in range(HEADS):
+            w1[h * 48 : h * 48 + 16, cols] = qkvT[256 + h * 16 : 272 + h * 16]
+            w1[h * 48 + 16 : h * 48 + 32, cols] = jnp.ones((16, HALF), BF)
+            w1[h * 48 + 32 : h * 48 + 48, cols] = qkvT[128 + h * 16 : 144 + h * 16]
+
     gain = gain_ref[...]
     gainc = jnp.sum(jnp.where(eye.astype(F32) > 0.5, gain, 0.0), axis=1, keepdims=True)
+    project(kept)
     wait_in(c1.at[pl.ds(0, NYC - 1)], 13)
-    wait_in(rx.at[pl.ds(0, SEQ - 1)], 4)
 
     def send_cot_z(t):
         zz, dev = z_peer(t)
@@ -198,28 +221,10 @@
 
     loop(NZ - 1, send_cot_z)
     c2[:, z] = c1[:, z]
+    wait_in(rx.at[pl.ds(0, SEQ - 1)], 4)
     patch[0:HALF, :] = rx[...].reshape(HALF, WIDTH)
-
-    xT = ntdot(eye, patch[...])
-    center = xT - jnp.mean(xT, axis=0, keepdims=True)
-    r = lax.rsqrt(jnp.mean(center * center, axis=0, keepdims=True) + 1e-5)
-    xh = center * r
-    xhT[...] = xh
-    rs[...] = jnp.broadcast_to(r, rs.shape)
-    nT = (xh * gainc).astype(BF)
-    nbT[...] = nT
-    mixed = dot(wqT, nT)
-    qkvT = mixed.astype(BF)
-    qT[...] = qkvT[0:128] * jnp.asarray(0.25, BF)
-    kT[...] = qkvT[128:256]
-    vT[...] = qkvT[256:384]
-    kf[...] = mixed[128:256].T.astype(BF)
-    vf[...] = mixed[256:384].T.astype(BF)
-    ones = jnp.ones((16, ROWS), BF)
-    for h in range(HEADS):
-        w1[h * 48 : h * 48 + 16, :] = qkvT[256 + h * 16 : 272 + h * 16]
-        w1[h * 48 + 16 : h * 48 + 32, :] = ones
-        w1[h * 48 + 32 : h * 48 + 48, :] = qkvT[128 + h * 16 : 144 + h * 16]
+    project(sent)
+
     head_of = iota((WIDTH, ROWS), 0) // 16
 
     def masked(ref, h):
@@ -302,19 +307,22 @@
         patch[cols, :] = (dxT.T + cotp[cols, :].astype(F32)).astype(BF)
         return jnp.sum(dnT * xh, axis=1, keepdims=True)
 
-    sent = slice(0, HALF)
-    kept = slice(HALF, ROWS)
-
     def back_sent(h, carry):
         do_wide = masked(doT, h)
         for c in range(4):
             ks = slice(c * 256, c * 256 + 256)
-            t = dot(vf[ks, :], do_wide)
-            xb[h, ks, :] = (eb[h, ks, :].astype(F32) * t).astype(BF)
+            cols = slice(0, ROWS) if c < 2 else sent
+            t = dot(vf[ks, :], do_wide[:, cols])
+            xb[h, ks, cols] = (eb[h, ks, cols].astype(F32) * t).astype(BF)
         backward(h, sent)
         return carry
 
     def back_kept(h, carry):
+        do_wide = masked(doT, h)[:, kept]
+        for c in range(2, 4):
+            ks = slice(c * 256, c * 256 + 256)
+            t = dot(vf[ks, :], do_wide)
+            xb[h, ks, kept] = (eb[h, ks, kept].astype(F32) * t).astype(BF)
         backward(h, kept)
         return carry
 
@@ -332,8 +340,8 @@
     ggT = ggT + input_grads(kept)
 
     for j, grad in enumerate((dqT, dkT, dvT)):
-        acc[j * 8 : j * 8 + 8] = ntdot(nbT[...], grad[...]).reshape(8, 16, WIDTH)
-    acc[24:32] = dot(attT[...], cotp[...]).reshape(8, 16, WIDTH)
+        acc[j * 8 : j * 8 + 8] = ntdot(nbT[...], grad[...]).astype(BF).reshape(8, 16, WIDTH)
+    acc[24:32] = dot(attT[...], cotp[...]).astype(BF).reshape(8, 16, WIDTH)
 
     def send_part(t):
         ww, dev = w_peer(t)
@@ -343,7 +351,7 @@
     rsb[w] = acc[w]
     gain_row = jnp.sum(jnp.where(eye.astype(F32) > 0.5, ggT, 0.0), axis=0, keepdims=True)
     wait_in(rsb.at[pl.ds(0, NW - 1)], 6)
-    part[...] = jnp.sum(rsb[...], axis=0)
+    part[...] = jnp.sum(rsb[...].astype(F32), axis=0).astype(BF)
 
     def send_part_z(t):
         push(part, zb.at[z], 7, z_peer(t)[1])
@@ -377,7 +385,7 @@
     tz[z] = tsum[...]
 
     wait_in(zb.at[pl.ds(0, NZ - 1)], 7)
-    full[...] = jnp.sum(zb[...], axis=0)
+    full[...] = jnp.sum(zb[...].astype(F32), axis=0)
 
     def send_full(t):
         push(full, fin.at[w], 11, w_peer(t)[1])
@@ -444,8 +452,8 @@
         vm(wide, BF), vm(wide, BF), vm(wide, BF), vm(wide, BF), vm(wide, F32), vm((8, ROWS), F32), vm(wide, BF),
         vm((2,) + sq, F32), vm((HEADS,) + sq, BF), vm((HEADS,) + sq, BF), vm((HEADS * 48, ROWS), BF), vm((2, 8, ROWS), F32),
         vm(wide, F32), vm(wide, F32), vm((HEADS, 8, ROWS), F32),
-        vm((ROWS + 16, WIDTH), F32), vm((NW, 16, WIDTH), F32), vm((NW, 16, WIDTH), F32), vm((16, WIDTH), F32),
-        vm((NZ, 16, WIDTH), F32), vm((16, WIDTH), F32), vm((NW, 16, WIDTH), F32),
+        vm((ROWS + 16, WIDTH), F32), vm((NW, 16, WIDTH), BF), vm((NW, 16, WIDTH), BF), vm((16, WIDTH), BF),
+        vm((NZ, 16, WIDTH), BF), vm((16, WIDTH), F32), vm((NW, 16, WIDTH), F32),
         vm((8, WIDTH), F32), vm((NW, 8, WIDTH), F32), vm((8, WIDTH), F32), vm((NZ, 8, WIDTH), F32),
         pltpu.SemaphoreType.DMA((15,)), pltpu.SemaphoreType.DMA((15,)),
     ]

time: 99.7 us -> 98.4 us (0.987)
  Pallas kernels: 98.9 us -> 97.6 us
    pallas_call x1, Pallas kernels: 96.5 us -> 95.2 us  [body(): pl.pallas_call(kernel, out_shape=(shape((ROWS + 32, WIDTH), BF), shape((H...]
where the time goes in v4:
time: 98.4 us; the launch traced here: 98.2 us
  Pallas kernels  97.6 us (99%)
    pallas_call x1, Pallas kernels, body(): pl.pallas_call(kernel, out_shape=(shape((ROWS + 32, WIDTH), BF), shape((H...  95.2 us
    pallas_call x1, Pallas kernels, body(): pl.pallas_call(finish, out_shape=(shape((1, ROWS, WIDTH), F32), shape((WI...  2.41 us

profile of v4, /device:TPU:1, one launch (start us, length us, event | category | flops | bytes accessed | tf_op | source)
XLA Modules:
  0.0 98.2 jit_solution(2760125305615986986)
XLA Ops:
  0.6 95.2 %shard_map.110 = (bf16[1056,128]{1,0:T(8,128)(2,1)}, f32[512,128]{1,0:T(8,128)}, f32[8,128]{1,0:T(8,128)}) custom-call(bf16[1,1024,128]{2,1,0:T(8,128)(2,1)} %pts_ref.1, bf16[1,1024,128]{2,1,0:T(8,128)(2,1)} %cot_ref.1, s32[1,1024]{1,0:T(1,128)} %order_ref.1, bf16[128,384]{1,0:T(8,128)(2,1)} %wqkv_ref.1, bf16[128,128]{1,0:T(8,128)(2,1)} %wout_ref.1, ...), custom_call_target="tpu_custom_call" | custom-call | tf_op jit(solution)/shard_map/pallas_call | solution.py:462
  95.8 2.4 %shard_map.111 = (f32[1,1024,128]{2,1,0:T(8,128)}, f32[128,384]{1,0:T(8,128)}, f32[128,128]{1,0:T(8,128)}, f32[1,128]{1,0:T(1,128)}, f32[7,128]{1,0:T(8,128)}) custom-call(bf16[1056,128]{1,0:T(8,128)(2,1)} %get-tuple-element.13.curve_ref, f32[512,128]{1,0:T(8,128)} %get-tuple-element.14.sums_ref, f32[8,128]{1,0:T(8,128)} %get-tuple-element.15.small_ref, ...), custom_call_target="tpu_custom_call" | custom-call | tf_op jit(solution)/shard_map/pallas_call | solution.py:472
